TPU v7x, 256 devices: a whole 4x4x8 slice. The times are simulated.
256 devices in a mesh: hist: 16 (over z, core), cand: 16 (over y, x).
Axes of the slice: x: 4, y: 4, z: 8, core: 2. Of those that a mesh axis runs over, the one named last changes fastest.
Arguments:
- history: bfloat16 [32, 256, 128, 512], P(None, 'hist', 'cand'), may hold values from -6 to 6
- candidates: bfloat16 [32, 2048, 512], P('hist', 'cand'), may hold values from -300 to 300
- selected: int32 [32, 16], replicated, may hold values from 0 to 255, as said below
- lengths: int32 [32], replicated, may hold values from 2048 to 32768
- kv_weight: bfloat16 [512, 1024], replicated, may hold values from -0.25 to 0.25
- query_weight: bfloat16 [512, 512], replicated, may hold values from -0.25 to 0.25
- out_weight: bfloat16 [512, 512], replicated, may hold values from -0.25 to 0.25
Outputs:
- interest: bfloat16 [32, 2048, 512], P('hist', 'cand')
Inputs may be any that keep to these rules, and one draw needn't show every extreme that they name: `selected`: each user's ids are distinct; at most 2 of a user's ids lie in one range [h * 16, (h + 1) * 16), exactly 2 in some range for every user; every user has an id below 16.
All inputs are finite; a program needn't handle non-finite values.
Results may differ from a plain program's by a relative error of at most 0.007.
The roundings to bfloat16 on the way count: a program that leaves them out, or rounds other values in their place, can miss the bound.
Values may be sent and summed in bfloat16 or wider, within the bound.
A program may use at most 128 MiB of HBM per device.

v0:
```python
import jax
import jax.numpy as jnp
from jax import lax
from jax.sharding import PartitionSpec as P

HEADS = 4
BLK = 128
NSEL = 16


def owner_slots(chosen, owner_index, per_owner, capacity):
    is_mine = chosen // per_owner == owner_index
    slot_rank = jnp.cumsum(is_mine.astype(jnp.int32), axis=1) - 1
    slot_hit = is_mine[:, :, None] & (
        slot_rank[:, :, None] == jnp.arange(capacity, dtype=jnp.int32)[None, None, :]
    )
    local_ids = jnp.sum(
        jnp.where(slot_hit, (chosen - owner_index * per_owner)[:, :, None], 0), axis=1
    )
    return local_ids


def project_rows(piece, kv_weight):
    return jnp.einsum("uskd,de->uske", piece, kv_weight, preferred_element_type=jnp.float32).astype(
        jnp.bfloat16
    )


def per_device(history, candidates, selected, lengths, kv_weight, query_weight, out_weight):
    owners = lax.axis_size("hist")
    owner_index = lax.axis_index("hist")
    users, per_owner, row_share, width = history.shape
    user_count, cand_count, cand_width = candidates.shape
    capacity = 2 * NSEL // owners
    local_ids = owner_slots(selected, owner_index, per_owner, capacity)
    picked = jnp.take_along_axis(history, local_ids[:, :, None, None], axis=1)
    arrived = lax.all_to_all(picked, "hist", split_axis=0, concat_axis=1, tiled=True)
    my_sel = lax.dynamic_slice_in_dim(selected, owner_index * user_count, user_count, 0)
    my_len = lax.dynamic_slice_in_dim(lengths, owner_index * user_count, user_count, 0)
    owner_ids = jnp.arange(owners, dtype=jnp.int32)
    match = (my_sel // per_owner)[:, None, :] == owner_ids[None, :, None]
    slot_rank = jnp.cumsum(match.astype(jnp.int32), axis=2) - 1
    slot_hit = match[..., None] & (slot_rank[..., None] == jnp.arange(capacity, dtype=jnp.int32))
    block_ids = jnp.sum(jnp.where(slot_hit, my_sel[:, None, :, None], 0), axis=2)
    slot_used = jnp.any(slot_hit, axis=2)
    positions = block_ids[..., None] * BLK + jnp.arange(BLK, dtype=jnp.int32)
    valid = slot_used[..., None] & (positions < my_len[:, None, None, None])
    key_count = owners * capacity * BLK
    valid = valid.reshape(user_count, key_count)
    kv_rows = project_rows(lax.all_gather(arrived, "cand", axis=2, tiled=True), kv_weight)
    head_size = width // HEADS
    kv_rows = kv_rows.reshape(user_count, key_count, 2, HEADS, head_size)
    key_part = kv_rows[:, :, 0]
    value_part = kv_rows[:, :, 1]
    queries = jnp.dot(
        candidates.reshape(user_count * cand_count, width),
        query_weight,
        preferred_element_type=jnp.float32,
    )
    queries = queries.astype(jnp.bfloat16).reshape(user_count, cand_count, HEADS, head_size)
    scores = jnp.einsum(
        "uchd,ukhd->uhck", queries, key_part, preferred_element_type=jnp.float32
    ) * head_size ** (-0.5)
    scores = jnp.where(valid[:, None, None, :], scores, jnp.float32(-1e30))
    largest = jnp.max(scores, axis=-1, keepdims=True)
    expo = jnp.exp(scores - largest)
    weights = (expo / jnp.sum(expo, axis=-1, keepdims=True)).astype(jnp.bfloat16)
    mixed = jnp.einsum("uhck,ukhd->uchd", weights, value_part, preferred_element_type=jnp.float32)
    mixed = mixed.reshape(user_count * cand_count, width).astype(jnp.bfloat16)
    interest = jnp.dot(mixed, out_weight, preferred_element_type=jnp.float32).astype(jnp.bfloat16)
    return interest.reshape(user_count, cand_count, width)


def solution(mesh):
    return jax.shard_map(
        per_device,
        mesh=mesh,
        in_specs=(P(None, "hist", "cand", None), P("hist", "cand", None), P(), P(), P(), P(), P()),
        out_specs=P("hist", "cand", None),
        check_vma=False,
    )
```

profile of v0, /device:TPU:1, one launch (start us, length us, event | category | flops | bytes accessed | tf_op | source)
XLA Modules:
  0.0 241.8 jit_solution(1613014819753839985)
XLA Ops:
  6.5 0.0 copy-start
  6.5 0.0 all-gather.2.cloned.1.call-start
  6.5 0.9 copy.34
  7.4 0.7 broadcast_subtract_fusion
  8.1 0.2 reduce_window_sum.22
  8.3 0.1 copy.39
  8.4 0.1 copy.38
  8.5 0.1 copy.40
  8.6 0.1 copy.41
  8.7 0.1 reshape.104
  8.8 2.9 %gather_fusion = bf16[64,8,512]{2,1,0:T(8,128)(2,1)S(1)} fusion(bf16[32,16,8,512]{3,2,1,0:T(8,128)(2,1)} %param.7, s32[64]{0:T(128)S(1)} %reshape.104), kind=kCustom, calls=%fused_computation | custom fusion | bytes 1049088 | tf_op jit(solution)/shard_map/jit(take_along_axis)/gather | solution.py:36
  11.7 0.1 broadcast_select_fusion
  11.9 27.1 %all_to_all.18 = bf16[32,2,8,512]{3,2,1,0:T(8,128)(2,1)S(1)} all-to-all(bf16[32,2,8,512]{3,2,1,0:T(8,128)(2,1)S(1)} %broadcast_select_fusion), channel_id=1, replica_groups=mesh['hist'=16,'cand'=16] {'hist'}, dimensions={0} | all-to-all | bytes 1048576 | tf_op jit(solution)/shard_map/all_to_all | solution.py:37
  38.9 0.9 copy.42
  39.8 0.0 all-gather.2.cloned.1.call-update
  39.9 0.7 dynamic_slice.7
  40.6 0.8 add_select_fusion.1
  41.4 0.1 copy.44
  41.4 0.1 copy.46
  41.5 0.4 reduce_window_sum.23
  41.9 0.2 fusion.19
  42.1 0.1 copy.45
  42.2 0.1 and.55
  42.3 0.1 select_reduce_fusion
  42.5 0.1 copy.47
  42.6 0.1 add.71
  42.7 1.4 convolution_convert_fusion.2
  44.1 0.1 reshape.102
  44.2 0.1 compare_and_fusion
  44.3 74.9 %all-gather.2.cloned.1.call-done = bf16[2,32,128,512]{3,2,1,0:T(8,128)(2,1)} async-done(((bf16[2,32,8,512]{3,2,1,0:T(8,128)(2,1)}), bf16[2,32,128,512]{3,2,1,0:T(8,128)(2,1)}) %all-gather.2.cloned.1.call-update) | async-done | bytes 8388624 | tf_op jit(solution)/shard_map/all_gather | solution.py:50
  119.2 0.0 copy-done
  119.2 15.8 %convolution_convert_fusion = bf16[2,32,128,1024]{3,2,1,0:T(8,128)(2,1)} fusion(bf16[2,32,128,512]{3,2,1,0:T(8,128)(2,1)} %all-gather.2.cloned.1.call-done, bf16[512,1024]{1,0:T(8,128)(2,1)S(1)} %copy-done), kind=kOutput, calls=%fused_computation.5 | convolution fusion | flops 8598323200 | bytes 26214400 | tf_op jit(solution)/shard_map/uskd,de->uske/dot_general | solution.py:24
  135.1 27.3 %reshape.100 = bf16[2,4096,2,4,128]{4,3,2,1,0:T(4,128)(2,1)} reshape(bf16[2,32,128,1024]{3,2,1,0:T(8,128)(2,1)} %convolution_convert_fusion) | data formatting | bytes 33554432 | tf_op jit(solution)/shard_map/reshape | solution.py:52
  162.4 15.6 %fusion.34 = (bf16[2,4096,1,4,128]{4,3,2,1,0:T(4,128)(2,1)}, bf16[2,4096,1,4,128]{4,3,2,1,0:T(4,128)(2,1)}) fusion(bf16[2,4096,2,4,128]{4,3,2,1,0:T(4,128)(2,1)} %reshape.100), kind=kLoop, calls=%fused_computation.62 | loop fusion | bytes 33554432 | tf_op jit(solution)/shard_map/slice | solution.py:54
  178.1 13.7 %copy.52 = bf16[2,4096,1,4,128]{1,4,3,0,2:T(8,128)(2,1)} copy(bf16[2,4096,1,4,128]{4,3,2,1,0:T(4,128)(2,1)} %get-tuple-element.9) | data formatting | bytes 16777216
  191.8 11.4 %fusion.2 = f32[2,4,128,4096]{3,2,1,0:T(8,128)} fusion(bf16[2,4096,1,4,128]{4,3,2,1,0:T(4,128)(2,1)} %get-tuple-element.10, bf16[2,128,4,128]{3,2,1,0:T(4,128)(2,1)S(1)} %reshape.102), kind=kOutput, calls=%fused_computation.8 | convolution fusion | flops 1073741824 | bytes 25427968 | tf_op jit(solution)/shard_map/uchd,ukhd->uhck/dot_general | solution.py:61
  203.2 19.8 %fusion.35 = (f32[2,4,128]{2,1,0:T(4,128)S(1)}, f32[2,4,128,4096]{3,2,1,0:T(8,128)}) fusion(f32[2,4,128,4096]{3,2,1,0:T(8,128)} %fusion.2, pred[2,4096]{1,0:T(4,128)(4,1)S(1)} %compare_and_fusion), kind=kOutput, calls=%fused_computation.63 | output fusion | flops 25169920 | bytes 33566720 | tf_op jit(solution)/shard_map/sub | solution.py:66
  223.0 0.0 copy-start.2
  223.0 0.0 copy-start.1
  223.0 10.7 %fusion.11 = bf16[2,128,4,128]{1,3,2,0:T(8,128)(2,1)S(1)} fusion(f32[2,4,128,4096]{3,2,1,0:T(8,128)} %get-tuple-element.14, f32[2,4,128]{2,1,0:T(4,128)S(1)} %get-tuple-element.13, bf16[2,4096,1,4,128]{1,4,3,0,2:T(8,128)(2,1)} %copy.52), kind=kOutput, calls=%fused_computation.17 | convolution fusion | flops 1082261504 | bytes 25432064 | tf_op jit(solution)/shard_map/uhck,ukhd->uchd/dot_general | solution.py:68
  233.7 0.2 copy.50
  233.9 0.0 copy-done.2
  233.9 1.0 convolution_convert_fusion.1
  234.9 0.0 copy-done.1
  (11 shorter events, 0.2 us)
Async XLA Ops:
  6.5 112.7 %copy-start = (bf16[512,1024]{1,0:T(8,128)(2,1)S(1)}, bf16[512,1024]{1,0:T(8,128)(2,1)}, u32[]{:S(2)}) copy-start(bf16[512,1024]{1,0:T(8,128)(2,1)} %param.11) | copy-start | bytes 3145732
  6.5 112.7 %all-gather.2.cloned.1.call-start = ((), (), s32[]{:S(2)}) async-start(), calls=%async_computation.1 | async-start | bytes 8912896 | tf_op jit(solution)/shard_map/all_gather | solution.py:50
  223.0 10.9 %copy-start.2 = (bf16[512,512]{1,0:T(8,128)(2,1)S(1)}, bf16[512,512]{1,0:T(8,128)(2,1)}, u32[]{:S(2)}) copy-start(bf16[512,512]{1,0:T(8,128)(2,1)} %param.13) | copy-start | bytes 1572868
  223.0 11.9 %copy-start.1 = (bf16[512,1024]{1,0:T(8,128)(2,1)S(1)}, bf16[512,1024]{1,0:T(8,128)(2,1)}, u32[]{:S(2)}) copy-start(bf16[512,1024]{1,0:T(8,128)(2,1)} %param.11) | copy-start | bytes 3145732
Sparse Core Ops, SparseCore 0:
  40.0 79.2 all-gather.1
where the time goes:
time: 243 us; the launch traced here: 242 us
  waiting for transfers between devices  74.9 us (31%)
  local copies, waits for them, and re-layouts  63.5 us (26%)
  matrix products  40.4 us (17%)
  blocking collectives  27.1 us (11%)
  other arithmetic  22.4 us (9%)
  between operations  13.5 us (6%)
    all_gather x1, waiting for transfers between devices, per_device(): lax.all_gather(arrived, 'cand', axis=2, tiled=True)  74.9 us
    reshape x1, local copies, waits for them, and re-layouts, per_device(): kv_rows = kv_rows.reshape(user_count, key_count, 2, HEADS, head_size)  27.3 us
    all_to_all x1, blocking collectives, per_device(): lax.all_to_all(picked, 'hist', split_axis=0, concat_axis=1, tiled=True)  27.1 us
    sub x1, other arithmetic, per_device(): expo = jnp.exp(scores - largest)  19.8 us
    dot_general x1, matrix products, project_rows(): jnp.einsum('uskd,de->uske', piece, kv_weight, preferred_element_type=jnp....  15.8 us
    slice x1, local copies, waits for them, and re-layouts, per_device(): value_part = kv_rows[:, :, 1]  15.6 us
    unnamed x8, local copies, waits for them, and re-layouts  14.6 us
    dot_general x1, matrix products, per_device(): jnp.einsum('uchd,ukhd->uhck', queries, key_part, preferred_element_type=j...  11.4 us
  transfers between devices with their start and end apart: 1, of which 1 were waited for; matrix products, arithmetic and copies ran while one was open for 2% of the time, Pallas kernels for 0%

commit v1 on v0

v1 whole, which is shorter than its diff:
```python
import functools

import jax
import jax.numpy as jnp
from jax import lax
from jax.experimental import pallas as pl
from jax.experimental.pallas import tpu as pltpu
from jax.sharding import PartitionSpec as P

MESH = pl.DeviceIdType.MESH
HEADS = 4
HD = 128
BLK = 128
NSEL = 16
D = 512
U = 32
LB = 16
OWN = 16
ROWS = 8
C = 128
SCALE = HD ** -0.5 * 1.4426950408889634
NT = (((1,), (1,)), ((), ()))


def kernel(sel_ref, len_ref, hist_hbm, cand_hbm, kvw_hbm, qw_hbm, ow_hbm, out_ref,
           hist_v, pick, zbuf0, zbuf1, cand_v, kvw, qw, ow, gat, qall, k_v, v_v, osend, ostat, orecv, rstat, ids,
           in_sem, zs_sem, zr_sem, xs_sem, xr_sem, qs_sem, qr_sem, os_sem, or_sem, ss_sem, sr_sem):
    zbuf = (zbuf0, zbuf1)
    h = lax.axis_index("hist")
    c = lax.axis_index("cand")
    z, core = h // 2, h % 2
    y, x = c // 4, c % 4

    hist_parts = 4
    per = U // hist_parts
    hist_copies = [
        pltpu.make_async_copy(hist_hbm.at[pl.ds(p * per, per)], hist_v.at[pl.ds(p * per, per)], in_sem.at[p])
        for p in range(hist_parts)
    ]
    for cp in hist_copies:
        cp.start()
    small = [
        pltpu.make_async_copy(cand_hbm, cand_v, in_sem.at[4]),
        pltpu.make_async_copy(qw_hbm, qw, in_sem.at[5]),
        pltpu.make_async_copy(kvw_hbm, kvw, in_sem.at[6]),
        pltpu.make_async_copy(ow_hbm, ow, in_sem.at[7]),
    ]
    for cp in small:
        cp.start()

    zpeers = []
    for dz in (4, 3, 5, 2, 6, 1, 7, 0):
        for dc in (0, 1):
            if dz == 0 and dc == 0:
                continue
            zpeers.append(lax.rem(z + dz, 8) * 2 + lax.rem(core + dc, 2))
    xpeers = [lax.rem(x + d, 4) for d in (2, 1, 3)]
    ypeers = [lax.rem(y + d, 4) for d in (2, 1, 3)]

    barrier = pltpu.get_barrier_semaphore()
    for hp in zpeers:
        pl.semaphore_signal(barrier, inc=1, device_id=(hp, c), device_id_type=MESH)
    for xp in xpeers:
        pl.semaphore_signal(barrier, inc=1, device_id=(h, y * 4 + xp), device_id_type=MESH)
    for yp in ypeers:
        pl.semaphore_signal(barrier, inc=1, device_id=(h, yp * 4 + x), device_id_type=MESH)

    def find(u, carry):
        first = jnp.int32(0)
        second = jnp.int32(0)
        for n in range(NSEL):
            one = sel_ref[u, n]
            mine = lax.shift_right_logical(one, 4) == h
            second = jnp.where(mine, first, second)
            first = jnp.where(mine, one & 15, first)
        ids[u, 0] = first
        ids[u, 1] = second
        return carry

    lax.fori_loop(0, U, find, 0)

    for cp in hist_copies:
        cp.wait()

    def choose(u, carry):
        top = hist_v[u, ids[u, 0]]
        low = hist_v[u, ids[u, 1]]
        pick[u] = jnp.concatenate([top, low], axis=0)
        return carry

    lax.fori_loop(0, U, choose, 0)

    pl.semaphore_wait(barrier, 21)

    for t in range(2):
        for hp in zpeers:
            pltpu.make_async_remote_copy(
                src_ref=pick.at[2 * hp + t], dst_ref=zbuf[t].at[h], send_sem=zs_sem.at[t], recv_sem=zr_sem.at[t],
                device_id=(hp, c), device_id_type=MESH,
            ).start()
        zbuf[t][h] = pick[2 * h + t]

    small[0].wait()
    small[1].wait()
    q_copies = []
    for t in range(2):
        qall[t, y] = jnp.dot(cand_v[t], qw[...], preferred_element_type=jnp.float32).astype(jnp.bfloat16)
        for i, yp in enumerate(ypeers):
            cp = pltpu.make_async_remote_copy(
                src_ref=qall.at[t, y], dst_ref=qall.at[t, y], send_sem=qs_sem.at[t, i], recv_sem=qr_sem.at[t, i],
                device_id=(h, yp * 4 + x), device_id_type=MESH,
            )
            cp.start()
            q_copies.append(cp)
    small[2].wait()
    small[3].wait()

    v_v[...] = jnp.ones_like(v_v)
    lane = lax.broadcasted_iota(jnp.int32, (1, 4 * C), 1)
    lane_n = lax.shift_right_logical(lane, 3) & 15
    lane_row = (y * 4 + lax.shift_right_logical(lane, 7)) * ROWS + (lane & 7)
    col = lax.broadcasted_iota(jnp.int32, (C, C), 1)

    all_copies = list(q_copies)
    for t in range(2):
        user = 2 * h + t
        sel = [sel_ref[user, n] for n in range(NSEL)]
        own = [lax.shift_right_logical(s, 4) for s in sel]
        slot = []
        for n in range(NSEL):
            later = jnp.int32(0)
            for m in range(n + 1, NSEL):
                later = later | (own[m] == own[n]).astype(jnp.int32)
            slot.append(later)
        idv = jnp.zeros((1, 4 * C), jnp.int32)
        for n in range(NSEL):
            idv = jnp.where(lane_n == n, sel[n], idv)
        bias = jnp.where(idv * BLK + lane_row < len_ref[user], 0.0, -1e30).astype(jnp.float32)

        pltpu.make_async_copy(zbuf[t].at[pl.ds(0, 15)], zbuf[t].at[pl.ds(0, 15)], zr_sem.at[t]).wait()
        for n in range(0, NSEL, 2):
            pair = []
            for m in (n, n + 1):
                both = zbuf[t][own[m]]
                pair.append(jnp.where(slot[m] == 0, both[:ROWS], both[ROWS:]))
            gat[t, x, n * ROWS:(n + 2) * ROWS] = jnp.concatenate(pair, axis=0)
        x_copies = []
        for i, xp in enumerate(xpeers):
            cp = pltpu.make_async_remote_copy(
                src_ref=gat.at[t, x], dst_ref=gat.at[t, x], send_sem=xs_sem.at[t, i], recv_sem=xr_sem.at[t, i],
                device_id=(h, y * 4 + xp), device_id_type=MESH,
            )
            cp.start()
            x_copies.append(cp)
        for cp in x_copies:
            cp.wait_recv()
        rows = gat[t].reshape(4 * C, D)
        k_v[...] = jnp.dot(rows, kvw[:, :D], preferred_element_type=jnp.float32).astype(jnp.bfloat16)
        values = jnp.dot(rows, kvw[:, D:], preferred_element_type=jnp.float32).astype(jnp.bfloat16)
        for hd in range(HEADS):
            v_v[:, hd * 256:hd * 256 + HD] = values[:, hd * HD:(hd + 1) * HD]
        for cp in q_copies[3 * t:3 * t + 3]:
            cp.wait_recv()

        def attend(yp):
            stat = jnp.zeros((C, C), jnp.float32)
            parts = []
            for hd in range(HEADS):
                s = lax.dot_general(
                    qall[t, yp, :, hd * HD:(hd + 1) * HD], k_v[:, hd * HD:(hd + 1) * HD], NT,
                    preferred_element_type=jnp.float32,
                ) * SCALE + bias
                m = jnp.max(s, axis=1, keepdims=True)
                p = jnp.exp2(s - m).astype(jnp.bfloat16)
                o = jnp.dot(p, v_v[:, hd * 256:(hd + 1) * 256], preferred_element_type=jnp.float32)
                l = o[:, HD:]
                parts.append((o[:, :HD] / l).astype(jnp.bfloat16))
                stat = jnp.where(col == hd, m, stat)
                stat = jnp.where(col == HEADS + hd, l, stat)
            return jnp.concatenate(parts, axis=1), stat.T[:8]

        for i, yp in enumerate(ypeers):
            part, stat = attend(yp)
            osend[t, i] = part
            ostat[t, i] = stat
            for src, dst, ssem, rsem in ((osend, orecv, os_sem, or_sem), (ostat, rstat, ss_sem, sr_sem)):
                cp = pltpu.make_async_remote_copy(
                    src_ref=src.at[t, i], dst_ref=dst.at[t, i], send_sem=ssem.at[t, i], recv_sem=rsem.at[t, i],
                    device_id=(h, yp * 4 + x), device_id_type=MESH,
                )
                cp.start()
                all_copies.append(cp)
        part, stat = attend(y)
        orecv[t, 3] = part
        rstat[t, 3] = stat
        for cp in x_copies:
            cp.wait_send()

    for cp in q_copies:
        cp.wait_send()
    out_copies = all_copies[6:]
    for t in range(2):
        for cp in out_copies[6 * t:6 * t + 6]:
            cp.wait_recv()
        stats = [rstat[t, k] for k in range(4)]
        top = jnp.maximum(jnp.maximum(stats[0][:4], stats[1][:4]), jnp.maximum(stats[2][:4], stats[3][:4]))
        parts = [s[4:] * jnp.exp2(s[:4] - top) for s in stats]
        total = (parts[0] + parts[1]) + (parts[2] + parts[3])
        wts = jnp.concatenate([p / total for p in parts] + [jnp.zeros((C - 16, C), jnp.float32)], axis=0).T
        mixed = []
        for hd in range(HEADS):
            acc = jnp.zeros((C, HD), jnp.float32)
            for k in range(4):
                acc = acc + wts[:, 4 * k + hd:4 * k + hd + 1] * orecv[t, k, :, hd * HD:(hd + 1) * HD].astype(jnp.float32)
            mixed.append(acc.astype(jnp.bfloat16))
        mixed = jnp.concatenate(mixed, axis=1)
        out_ref[t] = jnp.dot(mixed, ow[...], preferred_element_type=jnp.float32).astype(jnp.bfloat16)
    for cp in out_copies:
        cp.wait_send()
    for t in range(2):
        pltpu.make_async_copy(zbuf[t].at[pl.ds(0, 15)], zbuf[t].at[pl.ds(0, 15)], zs_sem.at[t]).wait()


def per_device(history, candidates, selected, lengths, kv_weight, query_weight, out_weight):
    smem = pl.BlockSpec(memory_space=pltpu.SMEM)
    any_ = pl.BlockSpec(memory_space=pl.ANY)
    bf = jnp.bfloat16
    dma = pltpu.SemaphoreType.DMA
    return pl.pallas_call(
        kernel,
        out_shape=jax.ShapeDtypeStruct((2, C, D), bf),
        in_specs=[smem, smem, any_, any_, any_, any_, any_],
        out_specs=pl.BlockSpec(memory_space=pltpu.VMEM),
        scratch_shapes=[
            pltpu.VMEM((U, LB, ROWS, D), bf),
            pltpu.VMEM((U, 2 * ROWS, D), bf),
            pltpu.VMEM((OWN, 2 * ROWS, D), bf),
            pltpu.VMEM((OWN, 2 * ROWS, D), bf),
            pltpu.VMEM((2, C, D), bf),
            pltpu.VMEM((D, 2 * D), bf),
            pltpu.VMEM((D, D), bf),
            pltpu.VMEM((D, D), bf),
            pltpu.VMEM((2, 4, C, D), bf),
            pltpu.VMEM((2, 4, C, D), bf),
            pltpu.VMEM((4 * C, D), bf),
            pltpu.VMEM((4 * C, HEADS * 256), bf),
            pltpu.VMEM((2, 3, C, D), bf),
            pltpu.VMEM((2, 3, 8, C), jnp.float32),
            pltpu.VMEM((2, 4, C, D), bf),
            pltpu.VMEM((2, 4, 8, C), jnp.float32),
            pltpu.SMEM((U, 2), jnp.int32),
            dma((8,)),
            dma((2,)), dma((2,)),
            dma((2, 3)), dma((2, 3)),
            dma((2, 3)), dma((2, 3)),
            dma((2, 3)), dma((2, 3)),
            dma((2, 3)), dma((2, 3)),
        ],
        compiler_params=pltpu.CompilerParams(
            collective_id=0, has_side_effects=True, vmem_limit_bytes=48 * 1024 * 1024
        ),
    )(selected, lengths, history, candidates, kv_weight, query_weight, out_weight)


def solution(mesh):
    return jax.shard_map(
        per_device,
        mesh=mesh,
        in_specs=(P(None, "hist", "cand", None), P("hist", "cand", None), P(), P(), P(), P(), P()),
        out_specs=P("hist", "cand", None),
        check_vma=False,
    )
```

time: 243 us -> 57.5 us (0.24)
  waiting for transfers between devices: 74.9 us -> 0 us
  local copies, waits for them, and re-layouts: 63.5 us -> 6.39 us
  Pallas kernels: 0 us -> 50.8 us
  matrix products: 40.4 us -> 0 us
  blocking collectives: 27.1 us -> 0 us
  other arithmetic: 22.4 us -> 0 us
  between operations: 13.5 us -> 0.01 us
    all_gather x1 -> x0, waiting for transfers between devices: 74.9 us -> none  [per_device(): lax.all_gather(arrived, 'cand', axis=2, tiled=True)]
    pallas_call x0 -> x1, Pallas kernels: none -> 50.8 us  [per_device(): pl.pallas_call(kernel, out_shape=jax.ShapeDtypeStruct((2, C, D), bf), in_...]
    dot_general x5 -> x0, matrix products: 40.4 us -> none  [the longest x1 15.8 us: project_rows(): jnp.einsum('uskd,de->uske', piece, kv_weight, preferred_element_type=jnp....]
    reshape x2 -> x0, local copies, waits for them, and re-layouts: 27.4 us -> none  [the longest x1 27.3 us: per_device(): kv_rows = kv_rows.reshape(user_count, key_count, 2, HEADS, head_size)]
    all_to_all x1 -> x0, blocking collectives: 27.1 us -> none  [per_device(): lax.all_to_all(picked, 'hist', split_axis=0, concat_axis=1, tiled=True)]
    sub x4 -> x0, other arithmetic: 20.5 us -> none  [the longest x1 19.8 us: per_device(): expo = jnp.exp(scores - largest)]
    slice x1 -> x0, local copies, waits for them, and re-layouts: 15.6 us -> none  [per_device(): value_part = kv_rows[:, :, 1]]
    unnamed x8 -> x12, local copies, waits for them, and re-layouts: 14.6 us -> 6.39 us
  transfers between devices with their start and end apart: 1 -> 0, of which waited for: 1 -> 0; matrix products, arithmetic and copies ran while one was open for 2% -> 0% of each run, Pallas kernels for 0% -> 0%
where the time goes in v1:
time: 57.5 us; the launch traced here: 57.2 us
  Pallas kernels  50.8 us (88%)
  local copies, waits for them, and re-layouts  6.39 us (11%)
    pallas_call x1, Pallas kernels, per_device(): pl.pallas_call(kernel, out_shape=jax.ShapeDtypeStruct((2, C, D), bf), in_...  50.8 us
    unnamed x12, local copies, waits for them, and re-layouts  6.39 us

profile of v1, /device:TPU:1, one launch (start us, length us, event | category | flops | bytes accessed | tf_op | source)
XLA Modules:
  0.0 57.2 jit_solution(10714595826515389276)
XLA Ops:
  0.0 0.8 %copy.8.sel_ref = s32[32,16]{1,0:T(8,128)S(1)} copy(s32[32,16]{0,1:T(8,128)} %param.9) | data formatting | bytes 4096 | tf_op args[2]
  0.8 0.0 copy-start
  0.8 1.2 %copy-done = bf16[512,1024]{1,0:T(8,128)(2,1)S(1)} copy-done((bf16[512,1024]{1,0:T(8,128)(2,1)S(1)}, bf16[512,1024]{1,0:T(8,128)(2,1)}, u32[]{:S(2)}) %copy-start) | copy-done | bytes 1048600
  2.0 0.0 copy-start.1
  2.0 1.0 %copy-done.1 = bf16[512,512]{1,0:T(8,128)(2,1)S(1)} copy-done((bf16[512,512]{1,0:T(8,128)(2,1)S(1)}, bf16[512,512]{1,0:T(8,128)(2,1)}, u32[]{:S(2)}) %copy-start.1) | copy-done | bytes 524312
  3.0 0.0 copy-start.2
  3.0 1.0 %copy-done.2 = bf16[512,512]{1,0:T(8,128)(2,1)S(1)} copy-done((bf16[512,512]{1,0:T(8,128)(2,1)S(1)}, bf16[512,512]{1,0:T(8,128)(2,1)}, u32[]{:S(2)}) %copy-start.2) | copy-done | bytes 524312
  4.1 0.0 copy-start.3
  4.1 0.9 %copy-done.3 = bf16[2,128,512]{2,1,0:T(8,128)(2,1)S(1)} copy-done((bf16[2,128,512]{2,1,0:T(8,128)(2,1)S(1)}, bf16[2,128,512]{2,1,0:T(8,128)(2,1)}, u32[]{:S(2)}) %copy-start.3) | copy-done | bytes 262168
  5.0 0.0 copy-start.4
  5.0 0.7 %copy-done.4 = s32[32]{0:T(128)S(1)} copy-done((s32[32]{0:T(128)S(1)}, s32[32]{0:T(128)}, u32[]{:S(2)}) %copy-start.4) | copy-done | bytes 152
  5.7 50.8 %shard_map.73 = bf16[2,128,512]{2,1,0:T(8,128)(2,1)S(1)} custom-call(s32[32,16]{1,0:T(8,128)S(1)} %copy.8.sel_ref, s32[32]{0:T(128)S(1)} %copy-done.4, bf16[32,16,8,512]{3,2,1,0:T(8,128)(2,1)} %hist_hbm.1, bf16[2,128,512]{2,1,0:T(8,128)(2,1)S(1)} %copy-done.3, bf16[512,1024]{1,0:T(8,128)(2,1)S(1)} %copy-done, bf16[512,512]{1,0:T(8,128)(2,1)S(1)} %copy-done.1, ...), custom_call_target="tpu_custom_call" | custom-call | tf_op jit(solution)/shard_map/pallas_call | solution.py:229
  56.5 0.7 %copy.10 = bf16[2,128,512]{2,1,0:T(8,128)(2,1)} copy(bf16[2,128,512]{2,1,0:T(8,128)(2,1)S(1)} %shard_map.73) | data formatting | bytes 524288
Async XLA Ops:
  0.8 1.2 %copy-start = (bf16[512,1024]{1,0:T(8,128)(2,1)S(1)}, bf16[512,1024]{1,0:T(8,128)(2,1)}, u32[]{:S(2)}) copy-start(bf16[512,1024]{1,0:T(8,128)(2,1)} %kvw_hbm.1) | copy-start | bytes 3145732
  2.0 1.0 %copy-start.1 = (bf16[512,512]{1,0:T(8,128)(2,1)S(1)}, bf16[512,512]{1,0:T(8,128)(2,1)}, u32[]{:S(2)}) copy-start(bf16[512,512]{1,0:T(8,128)(2,1)} %qw_hbm.1) | copy-start | bytes 1572868
  3.0 1.0 %copy-start.2 = (bf16[512,512]{1,0:T(8,128)(2,1)S(1)}, bf16[512,512]{1,0:T(8,128)(2,1)}, u32[]{:S(2)}) copy-start(bf16[512,512]{1,0:T(8,128)(2,1)} %ow_hbm.1) | copy-start | bytes 1572868
  4.1 0.9 %copy-start.3 = (bf16[2,128,512]{2,1,0:T(8,128)(2,1)S(1)}, bf16[2,128,512]{2,1,0:T(8,128)(2,1)}, u32[]{:S(2)}) copy-start(bf16[2,128,512]{2,1,0:T(8,128)(2,1)} %cand_hbm.1) | copy-start | bytes 786436
  5.0 0.7 %copy-start.4 = (s32[32]{0:T(128)S(1)}, s32[32]{0:T(128)}, u32[]{:S(2)}) copy-start(s32[32]{0:T(128)} %len_ref.1) | copy-start | bytes 388

commit v2 on v1

v2 whole, which is shorter than its diff:
```python
import jax
import jax.numpy as jnp
from jax import lax
from jax.experimental import pallas as pl
from jax.experimental.pallas import tpu as pltpu
from jax.sharding import PartitionSpec as P

MESH = pl.DeviceIdType.MESH
HEADS = 4
HD = 128
BLK = 128
NSEL = 16
D = 512
U = 32
LB = 16
OWN_RANGES = 16
ROWS = 8
C = 128
HALF = C // 2
SCALE = HD ** -0.5 * 1.4426950408889634
NT = (((1,), (1,)), ((), ()))
OPP, LEFT, RIGHT, OWN = 0, 1, 2, 3


def spread(buf, peers, send_sem, recv_sem):
    copies = [
        pltpu.make_async_remote_copy(
            src_ref=buf.at[OWN], dst_ref=buf.at[s], send_sem=send_sem.at[s], recv_sem=recv_sem.at[s],
            device_id=peers[s], device_id_type=MESH,
        )
        for s in (OPP, LEFT, RIGHT)
    ]

    def start():
        for cp in copies:
            cp.start()

    def arrived(*slots):
        for s in slots:
            copies[s].wait_recv()

    def sent():
        for cp in copies:
            cp.wait_send()

    return start, arrived, sent


def kernel(sel_ref, len_ref, hist_hbm, cand_hbm, kvw_hbm, qw_hbm, ow_hbm, out_ref,
           hist0, hist1, hist2, hist3, pick, zbuf0, zbuf1, cand_v, kvw, qw, ow, gat, qall, k_v, v_v,
           osend, ostat, orecv, rstat,
           in_sem, zs_sem, zr_sem, nb_sem, xs_sem, xr_sem, qs_sem, qr_sem, os_sem, or_sem, ss_sem, sr_sem):
    hist_v = (hist0, hist1, hist2, hist3)
    zbuf = (zbuf0, zbuf1)
    h = lax.axis_index("hist")
    c = lax.axis_index("cand")
    z, core = h // 2, h % 2
    y, x = c // 4, c % 4
    sibling = (2 * z + 1 - core, c)

    kpos = jnp.where(core == 0, x, y)
    cpos = jnp.where(core == 0, y, x)
    kstep = jnp.where(core == 0, 1, 4)
    cstep = 5 - kstep

    def kdev(d):
        return (h, cpos * cstep + ((kpos + d) & 3) * kstep)

    def cdev(d):
        return (h, ((cpos + d) & 3) * cstep + kpos * kstep)

    kpeers = {OPP: kdev(2), LEFT: kdev(1), RIGHT: kdev(3)}
    cpeers = {OPP: cdev(2), LEFT: cdev(1), RIGHT: cdev(3)}

    hist_copies = [
        pltpu.make_async_copy(hist_hbm.at[:, 2 * (p % 2) + p // 2], hist_v[p], in_sem.at[p]) for p in range(4)
    ]
    small = [
        pltpu.make_async_copy(cand_hbm, cand_v, in_sem.at[4]),
        pltpu.make_async_copy(qw_hbm, qw, in_sem.at[5]),
        pltpu.make_async_copy(kvw_hbm, kvw, in_sem.at[6]),
        pltpu.make_async_copy(ow_hbm, ow, in_sem.at[7]),
    ]
    for cp in hist_copies + small:
        cp.start()

    zorder = (4, 3, 5, 2, 6, 1, 7)
    zpeers = [lax.rem(z + dz, 8) for dz in zorder]

    barrier = pltpu.get_barrier_semaphore()
    for zp in zpeers:
        for k in range(2):
            pl.semaphore_signal(barrier, inc=1, device_id=(2 * zp + k, c), device_id_type=MESH)
    for dev in [sibling] + [f(d) for f in (kdev, cdev) for d in (2, 1, 3)]:
        pl.semaphore_signal(barrier, inc=1, device_id=dev, device_id_type=MESH)

    def choose(p):
        hist_copies[p].wait()

        def one_user(zp, carry):
            u = 4 * zp + 2 * (p % 2) + p // 2
            first = jnp.int32(0)
            second = jnp.int32(0)
            for n in range(NSEL):
                one = sel_ref[n, u]
                mine = lax.shift_right_logical(one, 4) == h
                second = jnp.where(mine, first, second)
                first = jnp.where(mine, one & 15, first)
            pick[p, zp] = jnp.concatenate([hist_v[p][zp, first], hist_v[p][zp, second]], axis=0)
            return carry

        lax.fori_loop(0, 8, one_user, 0)

    def zsend(p):
        for zp in zpeers:
            pltpu.make_async_remote_copy(
                src_ref=pick.at[p, zp], dst_ref=zbuf[p // 2].at[h], send_sem=zs_sem.at[p], recv_sem=zr_sem.at[p // 2],
                device_id=(2 * zp + p % 2, c), device_id_type=MESH,
            ).start()

    def zsent(p):
        pltpu.make_async_copy(zbuf0.at[pl.ds(0, 7)], zbuf0.at[pl.ds(0, 7)], zs_sem.at[p]).wait()

    nb_copies = [
        pltpu.make_async_remote_copy(
            src_ref=pick.at[2 * t + 1 - core, z], dst_ref=zbuf[t].at[h], send_sem=nb_sem.at[t], recv_sem=zr_sem.at[t],
            device_id=sibling, device_id_type=MESH,
        )
        for t in range(2)
    ]

    choose(0)
    pl.semaphore_wait(barrier, 21)
    zsend(0)
    choose(1)
    zsend(1)
    nb_copies[0].start()
    zbuf0[h] = pick[core, z]

    small[0].wait()
    small[1].wait()
    rows_to = [spread(gat.at[t], kpeers, xs_sem.at[t], xr_sem.at[t]) for t in range(2)]
    queries_to = [spread(qall.at[t], cpeers, qs_sem.at[t], qr_sem.at[t]) for t in range(2)]
    for t in range(2):
        qall[t, OWN] = jnp.dot(cand_v[t], qw[...], preferred_element_type=jnp.float32).astype(jnp.bfloat16)
        queries_to[t][0]()

    choose(2)
    choose(3)
    nb_copies[1].start()
    zbuf1[h] = pick[2 + core, z]

    zsent(0)
    zsend(2)

    v_v[...] = jnp.ones_like(v_v)
    lane = lax.broadcasted_iota(jnp.int32, (1, 4 * C), 1)
    lane_slot = lax.shift_right_logical(lane, 7)
    lane_n = lax.shift_right_logical(lane, 3) & 15
    lane_k = jnp.where(lane_slot == OPP, 2, jnp.where(lane_slot == LEFT, 3, jnp.where(lane_slot == RIGHT, 1, 0)))
    lane_row = (cpos * cstep + ((kpos + lane_k) & 3) * kstep) * ROWS + (lane & 7)
    col = lax.broadcasted_iota(jnp.int32, (2 * C, C), 1)

    def mask(t):
        user = 2 * h + t
        idv = jnp.zeros((1, 4 * C), jnp.int32)
        for n in range(NSEL):
            idv = jnp.where(lane_n == n, sel_ref[n, user], idv)
        return jnp.where(idv * BLK + lane_row < len_ref[user], 0.0, -1e30).astype(jnp.float32)

    def compact(t):
        user = 2 * h + t
        own = [lax.shift_right_logical(sel_ref[n, user], 4) for n in range(NSEL)]
        pltpu.make_async_copy(zbuf[t].at[pl.ds(0, 15)], zbuf[t].at[pl.ds(0, 15)], zr_sem.at[t]).wait()
        for n in range(0, NSEL, 2):
            pair = []
            for m in (n, n + 1):
                later = jnp.int32(0)
                for o in range(m + 1, NSEL):
                    later = later | (own[o] == own[m]).astype(jnp.int32)
                both = zbuf[t][own[m]]
                pair.append(jnp.where(later == 0, both[:ROWS], both[ROWS:]))
            gat[t, OWN, n * ROWS:(n + 2) * ROWS] = jnp.concatenate(pair, axis=0)

    def project(t, slots):
        for s in slots:
            kv = jnp.dot(gat[t, s], kvw[...], preferred_element_type=jnp.float32).astype(jnp.bfloat16)
            k_v[s * C:(s + 1) * C] = kv[:, :D]
            for hd in range(HEADS):
                v_v[s * C:(s + 1) * C, hd * 256:hd * 256 + HD] = kv[:, D + hd * HD:D + (hd + 1) * HD]

    out_copies = {}

    def send_out(t, s):
        to = cdev({OPP: 2, LEFT: 3, RIGHT: 1}[s])
        for kind, (src, dst, ssem, rsem) in enumerate(
            ((osend, orecv, os_sem, or_sem), (ostat, rstat, ss_sem, sr_sem))
        ):
            cp = pltpu.make_async_remote_copy(
                src_ref=src.at[t, s], dst_ref=dst.at[t, s], send_sem=ssem.at[t, s], recv_sem=rsem.at[t, s],
                device_id=to, device_id_type=MESH,
            )
            cp.start()
            out_copies[t, s, kind] = cp

    def attend(t, bias, pair):
        stat = jnp.zeros((2 * C, C), jnp.float32)
        parts = []
        for hd in range(HEADS):
            q = qall[t, pair:pair + 2, :, hd * HD:(hd + 1) * HD].reshape(2 * C, HD)
            s = lax.dot_general(q, k_v[:, hd * HD:(hd + 1) * HD], NT, preferred_element_type=jnp.float32) * SCALE + bias
            m = jnp.max(s, axis=1, keepdims=True)
            p = jnp.exp2(s - m).astype(jnp.bfloat16)
            o = jnp.dot(p, v_v[:, hd * 256:(hd + 1) * 256], preferred_element_type=jnp.float32)
            l = o[:, HD:]
            parts.append((o[:, :HD] / l).astype(jnp.bfloat16))
            stat = jnp.where(col == hd, m, stat)
            stat = jnp.where(col == HEADS + hd, l, stat)
        part = jnp.concatenate(parts, axis=1)
        stat = stat.T[:8]
        for i in range(2):
            s = pair + i
            if s == OWN:
                orecv[t, OWN] = part[i * C:(i + 1) * C]
                rstat[t, OWN] = stat[:, i * C:(i + 1) * C]
            else:
                osend[t, s] = part[i * C:(i + 1) * C]
                ostat[t, s] = stat[:, i * C:(i + 1) * C]
                send_out(t, s)

    def finish(t):
        for s in (OPP, LEFT, RIGHT):
            for kind in range(2):
                out_copies[t, s, kind].wait_recv()
        stats = [rstat[t, k] for k in range(4)]
        top = jnp.maximum(jnp.maximum(stats[0][:4], stats[1][:4]), jnp.maximum(stats[2][:4], stats[3][:4]))
        parts = [s[4:] * jnp.exp2(s[:4] - top) for s in stats]
        total = (parts[0] + parts[1]) + (parts[2] + parts[3])
        wts = jnp.concatenate([p / total for p in parts] + [jnp.zeros((C - 16, C), jnp.float32)], axis=0).T
        mixed = []
        for hd in range(HEADS):
            acc = jnp.zeros((C, HD), jnp.float32)
            for k in range(4):
                acc = acc + wts[:, 4 * k + hd:4 * k + hd + 1] * orecv[t, k, :, hd * HD:(hd + 1) * HD].astype(jnp.float32)
            mixed.append(acc.astype(jnp.bfloat16))
        mixed = jnp.concatenate(mixed, axis=1)
        out_ref[t] = jnp.dot(mixed, ow[...], preferred_element_type=jnp.float32).astype(jnp.bfloat16)

    bias0, bias1 = mask(0), mask(1)
    compact(0)
    rows_to[0][0]()
    zsent(1)
    zsend(3)
    small[2].wait()
    project(0, (OWN,))
    rows_to[0][1](LEFT, RIGHT)
    project(0, (LEFT, RIGHT))
    rows_to[0][1](OPP)
    project(0, (OPP,))
    queries_to[0][1](OPP, LEFT, RIGHT)
    attend(0, bias0, 0)
    compact(1)
    rows_to[1][0]()
    attend(0, bias0, 2)
    project(1, (OWN,))
    small[3].wait()
    finish(0)
    rows_to[1][1](LEFT, RIGHT)
    project(1, (LEFT, RIGHT))
    rows_to[1][1](OPP)
    project(1, (OPP,))
    queries_to[1][1](OPP, LEFT, RIGHT)
    attend(1, bias1, 0)
    attend(1, bias1, 2)
    finish(1)

    for t in range(2):
        rows_to[t][2]()
        queries_to[t][2]()
        zsent(2 + t)
        nb_copies[t].wait_send()
    for cp in out_copies.values():
        cp.wait_send()


def per_device(history, candidates, selected, lengths, kv_weight, query_weight, out_weight):
    smem = pl.BlockSpec(memory_space=pltpu.SMEM)
    any_ = pl.BlockSpec(memory_space=pl.ANY)
    bf = jnp.bfloat16
    dma = pltpu.SemaphoreType.DMA
    return pl.pallas_call(
        kernel,
        out_shape=jax.ShapeDtypeStruct((2, C, D), bf),
        in_specs=[smem, smem, any_, any_, any_, any_, any_],
        out_specs=pl.BlockSpec(memory_space=pltpu.VMEM),
        scratch_shapes=[pltpu.VMEM((8, LB, ROWS, D), bf)] * 4
        + [pltpu.VMEM((4, 8, 2 * ROWS, D), bf)]
        + [pltpu.VMEM((OWN_RANGES, 2 * ROWS, D), bf)] * 2
        + [
            pltpu.VMEM((2, C, D), bf),
            pltpu.VMEM((D, 2 * D), bf),
            pltpu.VMEM((D, D), bf),
            pltpu.VMEM((D, D), bf),
            pltpu.VMEM((2, 4, C, D), bf),
            pltpu.VMEM((2, 4, C, D), bf),
            pltpu.VMEM((4 * C, D), bf),
            pltpu.VMEM((4 * C, HEADS * 256), bf),
            pltpu.VMEM((2, 3, C, D), bf),
            pltpu.VMEM((2, 3, 8, C), jnp.float32),
            pltpu.VMEM((2, 4, C, D), bf),
            pltpu.VMEM((2, 4, 8, C), jnp.float32),
            dma((8,)),
            dma((4,)), dma((2,)), dma((2,)),
            dma((2, 3)), dma((2, 3)),
            dma((2, 3)), dma((2, 3)),
            dma((2, 3)), dma((2, 3)),
            dma((2, 3)), dma((2, 3)),
        ],
        compiler_params=pltpu.CompilerParams(
            collective_id=0, has_side_effects=True, vmem_limit_bytes=60 * 1024 * 1024
        ),
    )(selected.T, lengths, history.reshape(8, 4, LB, ROWS, D), candidates, kv_weight, query_weight, out_weight)


def solution(mesh):
    return jax.shard_map(
        per_device,
        mesh=mesh,
        in_specs=(P(None, "hist", "cand", None), P("hist", "cand", None), P(), P(), P(), P(), P()),
        out_specs=P("hist", "cand", None),
        check_vma=False,
    )
```

time: 57.5 us -> 45.2 us (0.79)
  Pallas kernels: 50.8 us -> 43.4 us
  local copies, waits for them, and re-layouts: 6.39 us -> 1.67 us
    pallas_call x1, Pallas kernels: 50.8 us -> 43.4 us  [per_device(): pl.pallas_call(kernel, out_shape=jax.ShapeDtypeStruct((2, C, D), bf), in_...]
    unnamed x12 -> x1, local copies, waits for them, and re-layouts: 6.39 us -> 1.67 us
where the time goes in v2:
time: 45.2 us; the launch traced here: 45 us
  Pallas kernels  43.4 us (96%)
  local copies, waits for them, and re-layouts  1.67 us (4%)
    pallas_call x1, Pallas kernels, per_device(): pl.pallas_call(kernel, out_shape=jax.ShapeDtypeStruct((2, C, D), bf), in_...  43.4 us
    unnamed x1, local copies, waits for them, and re-layouts  1.67 us

profile of v2, /device:TPU:1, one launch (start us, length us, event | category | flops | bytes accessed | tf_op | source)
XLA Modules:
  0.0 45.0 jit_solution(10255816440354018590)
XLA Ops:
  0.0 43.4 %shard_map.73 = bf16[2,128,512]{2,1,0:T(8,128)(2,1)} custom-call(s32[16,32]{1,0:T(8,128)} %bitcast.3, s32[32]{0:T(128)} %len_ref.1, bf16[8,4,16,8,512]{4,3,2,1,0:T(8,128)(2,1)} %bitcast.2, bf16[2,128,512]{2,1,0:T(8,128)(2,1)} %cand_hbm.1, bf16[512,1024]{1,0:T(8,128)(2,1)} %kvw_hbm.1, bf16[512,512]{1,0:T(8,128)(2,1)} %qw_hbm.1, bf16[512,512]{1,0:T(8,128)(2,1)} %ow_hbm.1), custom_call_target="tpu_custom_call" | custom-call | tf_op jit(solution)/shard_map/pallas_call | solution.py:291
  43.4 1.7 %copy.9 = bf16[2,128,512]{2,1,0:T(8,128)(2,1)} copy(bf16[2,128,512]{2,1,0:T(8,128)(2,1)} %shard_map.73) | data formatting | bytes 524288

commit v3 on v2

--- a/solution.py
+++ b/solution.py
@@ -191,7 +191,11 @@
 
     out_copies = {}
 
-    def send_out(t, s):
+    def send_out(t, *slots):
+        for s in slots:
+            send_one(t, s)
+
+    def send_one(t, s):
         to = cdev({OPP: 2, LEFT: 3, RIGHT: 1}[s])
         for kind, (src, dst, ssem, rsem) in enumerate(
             ((osend, orecv, os_sem, or_sem), (ostat, rstat, ss_sem, sr_sem))
@@ -226,7 +230,6 @@
             else:
                 osend[t, s] = part[i * C:(i + 1) * C]
                 ostat[t, s] = stat[:, i * C:(i + 1) * C]
-                send_out(t, s)
 
     def finish(t):
         for s in (OPP, LEFT, RIGHT):
@@ -247,35 +250,39 @@
         out_ref[t] = jnp.dot(mixed, ow[...], preferred_element_type=jnp.float32).astype(jnp.bfloat16)
 
     bias0, bias1 = mask(0), mask(1)
+    zsent(1)
+    zsend(3)
     compact(0)
     rows_to[0][0]()
-    zsent(1)
-    zsend(3)
     small[2].wait()
     project(0, (OWN,))
     rows_to[0][1](LEFT, RIGHT)
     project(0, (LEFT, RIGHT))
+    compact(1)
+    rows_to[1][0]()
     rows_to[0][1](OPP)
     project(0, (OPP,))
     queries_to[0][1](OPP, LEFT, RIGHT)
     attend(0, bias0, 0)
-    compact(1)
-    rows_to[1][0]()
     attend(0, bias0, 2)
+    rows_to[1][2]()
+    send_out(0, OPP, LEFT, RIGHT)
     project(1, (OWN,))
-    small[3].wait()
-    finish(0)
     rows_to[1][1](LEFT, RIGHT)
     project(1, (LEFT, RIGHT))
     rows_to[1][1](OPP)
     project(1, (OPP,))
     queries_to[1][1](OPP, LEFT, RIGHT)
     attend(1, bias1, 0)
+    send_out(1, OPP, LEFT)
     attend(1, bias1, 2)
+    send_out(1, RIGHT)
+    small[3].wait()
+    finish(0)
     finish(1)
 
+    rows_to[0][2]()
     for t in range(2):
-        rows_to[t][2]()
         queries_to[t][2]()
         zsent(2 + t)
         nb_copies[t].wait_send()

time: 45.2 us -> 42.3 us (0.936)
  Pallas kernels: 43.4 us -> 40.4 us
    pallas_call x1, Pallas kernels: 43.4 us -> 40.4 us  [per_device(): pl.pallas_call(kernel, out_shape=jax.ShapeDtypeStruct((2, C, D), bf), in_...]
where the time goes in v3:
time: 42.3 us; the launch traced here: 42.1 us
  Pallas kernels  40.4 us (96%)
  local copies, waits for them, and re-layouts  1.67 us (4%)
    pallas_call x1, Pallas kernels, per_device(): pl.pallas_call(kernel, out_shape=jax.ShapeDtypeStruct((2, C, D), bf), in_...  40.4 us
    unnamed x1, local copies, waits for them, and re-layouts  1.67 us

profile of v3, /device:TPU:1, one launch (start us, length us, event | category | flops | bytes accessed | tf_op | source)
XLA Modules:
  0.0 42.1 jit_solution(3390296926131739258)
XLA Ops:
  0.0 40.4 %shard_map.73 = bf16[2,128,512]{2,1,0:T(8,128)(2,1)} custom-call(s32[16,32]{1,0:T(8,128)} %bitcast.3, s32[32]{0:T(128)} %len_ref.1, bf16[8,4,16,8,512]{4,3,2,1,0:T(8,128)(2,1)} %bitcast.2, bf16[2,128,512]{2,1,0:T(8,128)(2,1)} %cand_hbm.1, bf16[512,1024]{1,0:T(8,128)(2,1)} %kvw_hbm.1, bf16[512,512]{1,0:T(8,128)(2,1)} %qw_hbm.1, bf16[512,512]{1,0:T(8,128)(2,1)} %ow_hbm.1), custom_call_target="tpu_custom_call" | custom-call | tf_op jit(solution)/shard_map/pallas_call | solution.py:298
  40.5 1.7 %copy.9 = bf16[2,128,512]{2,1,0:T(8,128)(2,1)} copy(bf16[2,128,512]{2,1,0:T(8,128)(2,1)} %shard_map.73) | data formatting | bytes 524288

commit v4 on v3

--- a/solution.py
+++ b/solution.py
@@ -19,36 +19,36 @@
 HALF = C // 2
 SCALE = HD ** -0.5 * 1.4426950408889634
 NT = (((1,), (1,)), ((), ()))
-OPP, LEFT, RIGHT, OWN = 0, 1, 2, 3
+OPP, OWN, LEFT, RIGHT = 0, 1, 2, 3
 
 
 def spread(buf, peers, send_sem, recv_sem):
-    copies = [
-        pltpu.make_async_remote_copy(
+    copies = {
+        s: pltpu.make_async_remote_copy(
             src_ref=buf.at[OWN], dst_ref=buf.at[s], send_sem=send_sem.at[s], recv_sem=recv_sem.at[s],
             device_id=peers[s], device_id_type=MESH,
         )
         for s in (OPP, LEFT, RIGHT)
-    ]
-
-    def start():
-        for cp in copies:
-            cp.start()
+    }
+
+    def start(*slots):
+        for s in slots:
+            copies[s].start()
 
     def arrived(*slots):
         for s in slots:
             copies[s].wait_recv()
 
     def sent():
-        for cp in copies:
+        for cp in copies.values():
             cp.wait_send()
 
     return start, arrived, sent
 
 
-def kernel(sel_ref, len_ref, hist_hbm, cand_hbm, kvw_hbm, qw_hbm, ow_hbm, out_ref,
+def kernel(meta_hbm, hist_hbm, cand_hbm, kvw_hbm, qw_hbm, ow_hbm, out_ref,
            hist0, hist1, hist2, hist3, pick, zbuf0, zbuf1, cand_v, kvw, qw, ow, gat, qall, k_v, v_v,
-           osend, ostat, orecv, rstat,
+           osend, ostat, orecv, rstat, sel_ref,
            in_sem, zs_sem, zr_sem, nb_sem, xs_sem, xr_sem, qs_sem, qr_sem, os_sem, or_sem, ss_sem, sr_sem):
     hist_v = (hist0, hist1, hist2, hist3)
     zbuf = (zbuf0, zbuf1)
@@ -81,7 +81,8 @@
         pltpu.make_async_copy(kvw_hbm, kvw, in_sem.at[6]),
         pltpu.make_async_copy(ow_hbm, ow, in_sem.at[7]),
     ]
-    for cp in hist_copies + small:
+    ids = pltpu.make_async_copy(meta_hbm, sel_ref, in_sem.at[8])
+    for cp in [ids] + hist_copies:
         cp.start()
 
     zorder = (4, 3, 5, 2, 6, 1, 7)
@@ -93,6 +94,10 @@
             pl.semaphore_signal(barrier, inc=1, device_id=(2 * zp + k, c), device_id_type=MESH)
     for dev in [sibling] + [f(d) for f in (kdev, cdev) for d in (2, 1, 3)]:
         pl.semaphore_signal(barrier, inc=1, device_id=dev, device_id_type=MESH)
+
+    for cp in small:
+        cp.start()
+    ids.wait()
 
     def choose(p):
         hist_copies[p].wait()
@@ -143,7 +148,7 @@
     queries_to = [spread(qall.at[t], cpeers, qs_sem.at[t], qr_sem.at[t]) for t in range(2)]
     for t in range(2):
         qall[t, OWN] = jnp.dot(cand_v[t], qw[...], preferred_element_type=jnp.float32).astype(jnp.bfloat16)
-        queries_to[t][0]()
+        queries_to[t][0](OPP, LEFT, RIGHT)
 
     choose(2)
     choose(3)
@@ -166,20 +171,25 @@
         idv = jnp.zeros((1, 4 * C), jnp.int32)
         for n in range(NSEL):
             idv = jnp.where(lane_n == n, sel_ref[n, user], idv)
-        return jnp.where(idv * BLK + lane_row < len_ref[user], 0.0, -1e30).astype(jnp.float32)
-
-    def compact(t):
-        user = 2 * h + t
-        own = [lax.shift_right_logical(sel_ref[n, user], 4) for n in range(NSEL)]
+        return jnp.where(idv * BLK + lane_row < sel_ref[NSEL, user], 0.0, -1e30).astype(jnp.float32)
+
+    def places(t):
+        own = [lax.shift_right_logical(sel_ref[n, 2 * h + t], 4) for n in range(NSEL)]
+        second = []
+        for n in range(NSEL):
+            later = jnp.int32(0)
+            for o in range(n + 1, NSEL):
+                later = later | (own[o] == own[n]).astype(jnp.int32)
+            second.append(later)
+        return own, second
+
+    def compact(t, own, second):
         pltpu.make_async_copy(zbuf[t].at[pl.ds(0, 15)], zbuf[t].at[pl.ds(0, 15)], zr_sem.at[t]).wait()
         for n in range(0, NSEL, 2):
             pair = []
             for m in (n, n + 1):
-                later = jnp.int32(0)
-                for o in range(m + 1, NSEL):
-                    later = later | (own[o] == own[m]).astype(jnp.int32)
                 both = zbuf[t][own[m]]
-                pair.append(jnp.where(later == 0, both[:ROWS], both[ROWS:]))
+                pair.append(jnp.where(second[m] == 0, both[:ROWS], both[ROWS:]))
             gat[t, OWN, n * ROWS:(n + 2) * ROWS] = jnp.concatenate(pair, axis=0)
 
     def project(t, slots):
@@ -216,10 +226,9 @@
             m = jnp.max(s, axis=1, keepdims=True)
             p = jnp.exp2(s - m).astype(jnp.bfloat16)
             o = jnp.dot(p, v_v[:, hd * 256:(hd + 1) * 256], preferred_element_type=jnp.float32)
-            l = o[:, HD:]
-            parts.append((o[:, :HD] / l).astype(jnp.bfloat16))
+            parts.append(o[:, :HD].astype(jnp.bfloat16))
             stat = jnp.where(col == hd, m, stat)
-            stat = jnp.where(col == HEADS + hd, l, stat)
+            stat = jnp.where(col == HEADS + hd, o[:, HD:], stat)
         part = jnp.concatenate(parts, axis=1)
         stat = stat.T[:8]
         for i in range(2):
@@ -237,8 +246,9 @@
                 out_copies[t, s, kind].wait_recv()
         stats = [rstat[t, k] for k in range(4)]
         top = jnp.maximum(jnp.maximum(stats[0][:4], stats[1][:4]), jnp.maximum(stats[2][:4], stats[3][:4]))
-        parts = [s[4:] * jnp.exp2(s[:4] - top) for s in stats]
-        total = (parts[0] + parts[1]) + (parts[2] + parts[3])
+        parts = [jnp.exp2(s[:4] - top) for s in stats]
+        sums = [p * s[4:] for p, s in zip(parts, stats)]
+        total = (sums[0] + sums[1]) + (sums[2] + sums[3])
         wts = jnp.concatenate([p / total for p in parts] + [jnp.zeros((C - 16, C), jnp.float32)], axis=0).T
         mixed = []
         for hd in range(HEADS):
@@ -250,16 +260,17 @@
         out_ref[t] = jnp.dot(mixed, ow[...], preferred_element_type=jnp.float32).astype(jnp.bfloat16)
 
     bias0, bias1 = mask(0), mask(1)
+    places0, places1 = places(0), places(1)
     zsent(1)
     zsend(3)
-    compact(0)
-    rows_to[0][0]()
+    compact(0, *places0)
+    rows_to[0][0](OPP, LEFT, RIGHT)
     small[2].wait()
     project(0, (OWN,))
+    compact(1, *places1)
+    rows_to[1][0](OPP, LEFT, RIGHT)
     rows_to[0][1](LEFT, RIGHT)
     project(0, (LEFT, RIGHT))
-    compact(1)
-    rows_to[1][0]()
     rows_to[0][1](OPP)
     project(0, (OPP,))
     queries_to[0][1](OPP, LEFT, RIGHT)
@@ -274,9 +285,9 @@
     project(1, (OPP,))
     queries_to[1][1](OPP, LEFT, RIGHT)
     attend(1, bias1, 0)
-    send_out(1, OPP, LEFT)
+    send_out(1, OPP)
     attend(1, bias1, 2)
-    send_out(1, RIGHT)
+    send_out(1, LEFT, RIGHT)
     small[3].wait()
     finish(0)
     finish(1)
@@ -291,14 +302,13 @@
 
 
 def per_device(history, candidates, selected, lengths, kv_weight, query_weight, out_weight):
-    smem = pl.BlockSpec(memory_space=pltpu.SMEM)
     any_ = pl.BlockSpec(memory_space=pl.ANY)
     bf = jnp.bfloat16
     dma = pltpu.SemaphoreType.DMA
     return pl.pallas_call(
         kernel,
         out_shape=jax.ShapeDtypeStruct((2, C, D), bf),
-        in_specs=[smem, smem, any_, any_, any_, any_, any_],
+        in_specs=[any_] * 6,
         out_specs=pl.BlockSpec(memory_space=pltpu.VMEM),
         scratch_shapes=[pltpu.VMEM((8, LB, ROWS, D), bf)] * 4
         + [pltpu.VMEM((4, 8, 2 * ROWS, D), bf)]
@@ -312,21 +322,22 @@
             pltpu.VMEM((2, 4, C, D), bf),
             pltpu.VMEM((4 * C, D), bf),
             pltpu.VMEM((4 * C, HEADS * 256), bf),
-            pltpu.VMEM((2, 3, C, D), bf),
-            pltpu.VMEM((2, 3, 8, C), jnp.float32),
             pltpu.VMEM((2, 4, C, D), bf),
             pltpu.VMEM((2, 4, 8, C), jnp.float32),
-            dma((8,)),
+            pltpu.VMEM((2, 4, C, D), bf),
+            pltpu.VMEM((2, 4, 8, C), jnp.float32),
+            pltpu.SMEM((NSEL + 1, U), jnp.int32),
+            dma((9,)),
             dma((4,)), dma((2,)), dma((2,)),
-            dma((2, 3)), dma((2, 3)),
-            dma((2, 3)), dma((2, 3)),
-            dma((2, 3)), dma((2, 3)),
-            dma((2, 3)), dma((2, 3)),
+            dma((2, 4)), dma((2, 4)),
+            dma((2, 4)), dma((2, 4)),
+            dma((2, 4)), dma((2, 4)),
+            dma((2, 4)), dma((2, 4)),
         ],
         compiler_params=pltpu.CompilerParams(
-            collective_id=0, has_side_effects=True, vmem_limit_bytes=60 * 1024 * 1024
+            collective_id=0, has_side_effects=True, vmem_limit_bytes=56098816
         ),
-    )(selected.T, lengths, history.reshape(8, 4, LB, ROWS, D), candidates, kv_weight, query_weight, out_weight)
+    )(jnp.concatenate([selected.T, lengths[None]], axis=0), history.reshape(8, 4, LB, ROWS, D), candidates, kv_weight, query_weight, out_weight)
 
 
 def solution(mesh):

time: 42.3 us -> 39.6 us (0.936)
  Pallas kernels: 40.4 us -> 38 us
  local copies, waits for them, and re-layouts: 1.67 us -> 0.71 us
  other arithmetic: 0 us -> 0.72 us
    pallas_call x1, Pallas kernels: 40.4 us -> 38 us  [per_device(): pl.pallas_call(kernel, out_shape=jax.ShapeDtypeStruct((2, C, D), bf), in_...]
    unnamed x1, local copies, waits for them, and re-layouts: 1.67 us -> 0.71 us
    concatenate x0 -> x1, other arithmetic: none -> 0.72 us  [per_device(): jnp.concatenate([selected.T, lengths[None]], axis=0)]
where the time goes in v4:
time: 39.6 us; the launch traced here: 39.5 us
  Pallas kernels  38 us (96%)
  other arithmetic  0.72 us (2%)
  local copies, waits for them, and re-layouts  0.71 us (2%)
    pallas_call x1, Pallas kernels, per_device(): pl.pallas_call(kernel, out_shape=jax.ShapeDtypeStruct((2, C, D), bf), in_...  38 us

profile of v4, /device:TPU:1, one launch (start us, length us, event | category | flops | bytes accessed | tf_op | source)
XLA Modules:
  0.0 39.5 jit_solution(9647826781865252441)
XLA Ops:
  0.0 0.7 %pad_add_fusion.meta_hbm = s32[17,32]{1,0:T(8,128)S(1)} fusion(s32[1,32]{1,0:T(1,128)} %bitcast.5, s32[16,32]{1,0:T(8,128)} %bitcast.4), kind=kLoop, calls=%fused_computation | loop fusion | flops 544 | bytes 4352 | tf_op jit(solution)/shard_map/concatenate | solution.py:340
  0.7 38.0 %shard_map.73 = bf16[2,128,512]{2,1,0:T(8,128)(2,1)S(1)} custom-call(s32[17,32]{1,0:T(8,128)S(1)} %pad_add_fusion.meta_hbm, bf16[8,4,16,8,512]{4,3,2,1,0:T(8,128)(2,1)} %bitcast.3, bf16[2,128,512]{2,1,0:T(8,128)(2,1)} %cand_hbm.1, bf16[512,1024]{1,0:T(8,128)(2,1)} %kvw_hbm.1, bf16[512,512]{1,0:T(8,128)(2,1)} %qw_hbm.1, bf16[512,512]{1,0:T(8,128)(2,1)} %ow_hbm.1), custom_call_target="tpu_custom_call" | custom-call | tf_op jit(solution)/shard_map/pallas_call | solution.py:308
  38.7 0.7 %copy.9 = bf16[2,128,512]{2,1,0:T(8,128)(2,1)} copy(bf16[2,128,512]{2,1,0:T(8,128)(2,1)S(1)} %shard_map.73) | data formatting | bytes 524288

commit v5 on v4

--- a/solution.py
+++ b/solution.py
@@ -19,28 +19,29 @@
 HALF = C // 2
 SCALE = HD ** -0.5 * 1.4426950408889634
 NT = (((1,), (1,)), ((), ()))
-OPP, OWN, LEFT, RIGHT = 0, 1, 2, 3
+OPP, LEFT, RIGHT, OWN = 0, 1, 2, 3
+OFFSET = {OPP: 2, LEFT: 3, RIGHT: 1}
 
 
 def spread(buf, peers, send_sem, recv_sem):
-    copies = {
-        s: pltpu.make_async_remote_copy(
+    copies = [
+        pltpu.make_async_remote_copy(
             src_ref=buf.at[OWN], dst_ref=buf.at[s], send_sem=send_sem.at[s], recv_sem=recv_sem.at[s],
             device_id=peers[s], device_id_type=MESH,
         )
         for s in (OPP, LEFT, RIGHT)
-    }
-
-    def start(*slots):
-        for s in slots:
-            copies[s].start()
+    ]
+
+    def start():
+        for cp in copies:
+            cp.start()
 
     def arrived(*slots):
         for s in slots:
             copies[s].wait_recv()
 
     def sent():
-        for cp in copies.values():
+        for cp in copies:
             cp.wait_send()
 
     return start, arrived, sent
@@ -148,7 +149,7 @@
     queries_to = [spread(qall.at[t], cpeers, qs_sem.at[t], qr_sem.at[t]) for t in range(2)]
     for t in range(2):
         qall[t, OWN] = jnp.dot(cand_v[t], qw[...], preferred_element_type=jnp.float32).astype(jnp.bfloat16)
-        queries_to[t][0](OPP, LEFT, RIGHT)
+        queries_to[t][0]()
 
     choose(2)
     choose(3)
@@ -164,7 +165,7 @@
     lane_n = lax.shift_right_logical(lane, 3) & 15
     lane_k = jnp.where(lane_slot == OPP, 2, jnp.where(lane_slot == LEFT, 3, jnp.where(lane_slot == RIGHT, 1, 0)))
     lane_row = (cpos * cstep + ((kpos + lane_k) & 3) * kstep) * ROWS + (lane & 7)
-    col = lax.broadcasted_iota(jnp.int32, (2 * C, C), 1)
+    col = lax.broadcasted_iota(jnp.int32, (4 * C, C), 1)
 
     def mask(t):
         user = 2 * h + t
@@ -199,105 +200,108 @@
             for hd in range(HEADS):
                 v_v[s * C:(s + 1) * C, hd * 256:hd * 256 + HD] = kv[:, D + hd * HD:D + (hd + 1) * HD]
 
-    out_copies = {}
-
-    def send_out(t, *slots):
-        for s in slots:
-            send_one(t, s)
-
-    def send_one(t, s):
-        to = cdev({OPP: 2, LEFT: 3, RIGHT: 1}[s])
-        for kind, (src, dst, ssem, rsem) in enumerate(
-            ((osend, orecv, os_sem, or_sem), (ostat, rstat, ss_sem, sr_sem))
-        ):
+    out_copies = [[], []]
+
+    def send_out(t, heads):
+        for s in (OPP, LEFT, RIGHT):
             cp = pltpu.make_async_remote_copy(
-                src_ref=src.at[t, s], dst_ref=dst.at[t, s], send_sem=ssem.at[t, s], recv_sem=rsem.at[t, s],
-                device_id=to, device_id_type=MESH,
+                src_ref=osend.at[t, s, heads], dst_ref=orecv.at[t, s, heads],
+                send_sem=os_sem.at[t, s, heads.start], recv_sem=or_sem.at[t, s, heads.start],
+                device_id=cdev(OFFSET[s]), device_id_type=MESH,
             )
             cp.start()
-            out_copies[t, s, kind] = cp
-
-    def attend(t, bias, pair):
-        stat = jnp.zeros((2 * C, C), jnp.float32)
-        parts = []
+            out_copies[t].append(cp)
+
+    def send_stat(t, heads):
+        for s in (OPP, LEFT, RIGHT):
+            cp = pltpu.make_async_remote_copy(
+                src_ref=ostat.at[t, s, heads], dst_ref=rstat.at[t, s, heads],
+                send_sem=ss_sem.at[t, s, heads.start], recv_sem=sr_sem.at[t, s, heads.start],
+                device_id=cdev(OFFSET[s]), device_id_type=MESH,
+            )
+            cp.start()
+            out_copies[t].append(cp)
+
+    def attend(t, bias, after_head):
         for hd in range(HEADS):
-            q = qall[t, pair:pair + 2, :, hd * HD:(hd + 1) * HD].reshape(2 * C, HD)
+            q = qall[t, :, :, hd * HD:(hd + 1) * HD].reshape(4 * C, HD)
             s = lax.dot_general(q, k_v[:, hd * HD:(hd + 1) * HD], NT, preferred_element_type=jnp.float32) * SCALE + bias
             m = jnp.max(s, axis=1, keepdims=True)
             p = jnp.exp2(s - m).astype(jnp.bfloat16)
             o = jnp.dot(p, v_v[:, hd * 256:(hd + 1) * 256], preferred_element_type=jnp.float32)
-            parts.append(o[:, :HD].astype(jnp.bfloat16))
-            stat = jnp.where(col == hd, m, stat)
-            stat = jnp.where(col == HEADS + hd, o[:, HD:], stat)
-        part = jnp.concatenate(parts, axis=1)
-        stat = stat.T[:8]
-        for i in range(2):
-            s = pair + i
-            if s == OWN:
-                orecv[t, OWN] = part[i * C:(i + 1) * C]
-                rstat[t, OWN] = stat[:, i * C:(i + 1) * C]
-            else:
-                osend[t, s] = part[i * C:(i + 1) * C]
-                ostat[t, s] = stat[:, i * C:(i + 1) * C]
-
-    def finish(t):
-        for s in (OPP, LEFT, RIGHT):
-            for kind in range(2):
-                out_copies[t, s, kind].wait_recv()
-        stats = [rstat[t, k] for k in range(4)]
-        top = jnp.maximum(jnp.maximum(stats[0][:4], stats[1][:4]), jnp.maximum(stats[2][:4], stats[3][:4]))
-        parts = [jnp.exp2(s[:4] - top) for s in stats]
-        sums = [p * s[4:] for p, s in zip(parts, stats)]
-        total = (sums[0] + sums[1]) + (sums[2] + sums[3])
-        wts = jnp.concatenate([p / total for p in parts] + [jnp.zeros((C - 16, C), jnp.float32)], axis=0).T
-        mixed = []
+            part = o[:, :HD].astype(jnp.bfloat16)
+            stat = jnp.where(col == 0, m, o[:, HD:]).T[:8]
+            for i in range(4):
+                dst = orecv if i == OWN else osend
+                dst[t, i, hd] = part[i * C:(i + 1) * C]
+                dst = rstat if i == OWN else ostat
+                dst[t, i, hd] = stat[:, i * C:(i + 1) * C]
+            after_head(hd)
+
+    def finish(t, by_head):
+        acc = jnp.zeros((C, D), jnp.float32)
+        if not by_head:
+            for cp in out_copies[t]:
+                cp.wait_recv()
         for hd in range(HEADS):
-            acc = jnp.zeros((C, HD), jnp.float32)
+            if by_head:
+                for cp in out_copies[t][6 * hd:6 * hd + 6]:
+                    cp.wait_recv()
+            stats = [rstat[t, k, hd] for k in range(4)]
+            top = jnp.maximum(jnp.maximum(stats[0][:1], stats[1][:1]), jnp.maximum(stats[2][:1], stats[3][:1]))
+            parts = [jnp.exp2(s[:1] - top) for s in stats]
+            sums = [p * s[1:2] for p, s in zip(parts, stats)]
+            total = (sums[0] + sums[1]) + (sums[2] + sums[3])
+            wts = jnp.concatenate([p / total for p in parts] + [jnp.zeros((C - 4, C), jnp.float32)], axis=0).T
+            mixed = jnp.zeros((C, HD), jnp.float32)
             for k in range(4):
-                acc = acc + wts[:, 4 * k + hd:4 * k + hd + 1] * orecv[t, k, :, hd * HD:(hd + 1) * HD].astype(jnp.float32)
-            mixed.append(acc.astype(jnp.bfloat16))
-        mixed = jnp.concatenate(mixed, axis=1)
-        out_ref[t] = jnp.dot(mixed, ow[...], preferred_element_type=jnp.float32).astype(jnp.bfloat16)
+                mixed = mixed + wts[:, k:k + 1] * orecv[t, k, hd].astype(jnp.float32)
+            acc = acc + jnp.dot(
+                mixed.astype(jnp.bfloat16), ow[hd * HD:(hd + 1) * HD], preferred_element_type=jnp.float32
+            )
+        out_ref[t] = acc.astype(jnp.bfloat16)
 
     bias0, bias1 = mask(0), mask(1)
     places0, places1 = places(0), places(1)
     zsent(1)
     zsend(3)
     compact(0, *places0)
-    rows_to[0][0](OPP, LEFT, RIGHT)
+    rows_to[0][0]()
     small[2].wait()
     project(0, (OWN,))
     compact(1, *places1)
-    rows_to[1][0](OPP, LEFT, RIGHT)
+    rows_to[1][0]()
     rows_to[0][1](LEFT, RIGHT)
     project(0, (LEFT, RIGHT))
     rows_to[0][1](OPP)
     project(0, (OPP,))
     queries_to[0][1](OPP, LEFT, RIGHT)
-    attend(0, bias0, 0)
-    attend(0, bias0, 2)
+    attend(0, bias0, lambda hd: None)
     rows_to[1][2]()
-    send_out(0, OPP, LEFT, RIGHT)
+    send_out(0, pl.ds(0, HEADS))
+    send_stat(0, pl.ds(0, HEADS))
     project(1, (OWN,))
     rows_to[1][1](LEFT, RIGHT)
     project(1, (LEFT, RIGHT))
     rows_to[1][1](OPP)
     project(1, (OPP,))
     queries_to[1][1](OPP, LEFT, RIGHT)
-    attend(1, bias1, 0)
-    send_out(1, OPP)
-    attend(1, bias1, 2)
-    send_out(1, LEFT, RIGHT)
+
+    def send_head(hd):
+        send_stat(1, pl.ds(hd, 1))
+        send_out(1, pl.ds(hd, 1))
+
+    attend(1, bias1, send_head)
     small[3].wait()
-    finish(0)
-    finish(1)
+    finish(0, False)
+    finish(1, True)
 
     rows_to[0][2]()
     for t in range(2):
         queries_to[t][2]()
         zsent(2 + t)
         nb_copies[t].wait_send()
-    for cp in out_copies.values():
+    for cp in out_copies[0] + out_copies[1]:
         cp.wait_send()
 
 
@@ -322,17 +326,17 @@
             pltpu.VMEM((2, 4, C, D), bf),
             pltpu.VMEM((4 * C, D), bf),
             pltpu.VMEM((4 * C, HEADS * 256), bf),
-            pltpu.VMEM((2, 4, C, D), bf),
-            pltpu.VMEM((2, 4, 8, C), jnp.float32),
-            pltpu.VMEM((2, 4, C, D), bf),
-            pltpu.VMEM((2, 4, 8, C), jnp.float32),
+            pltpu.VMEM((2, 3, HEADS, C, HD), bf),
+            pltpu.VMEM((2, 3, HEADS, 8, C), jnp.float32),
+            pltpu.VMEM((2, 4, HEADS, C, HD), bf),
+            pltpu.VMEM((2, 4, HEADS, 8, C), jnp.float32),
             pltpu.SMEM((NSEL + 1, U), jnp.int32),
             dma((9,)),
             dma((4,)), dma((2,)), dma((2,)),
-            dma((2, 4)), dma((2, 4)),
-            dma((2, 4)), dma((2, 4)),
-            dma((2, 4)), dma((2, 4)),
-            dma((2, 4)), dma((2, 4)),
+            dma((2, 3)), dma((2, 3)),
+            dma((2, 3)), dma((2, 3)),
+            dma((2, 3, HEADS)), dma((2, 3, HEADS)),
+            dma((2, 3, HEADS)), dma((2, 3, HEADS)),
         ],
         compiler_params=pltpu.CompilerParams(
             collective_id=0, has_side_effects=True, vmem_limit_bytes=56098816

time: 39.6 us -> 39.6 us (level)
  no operation moved by 1% of the time
where the time goes in v5:
time: 39.6 us; the launch traced here: 39.5 us
  Pallas kernels  38 us (96%)
  other arithmetic  0.72 us (2%)
  local copies, waits for them, and re-layouts  0.71 us (2%)
    pallas_call x1, Pallas kernels, per_device(): pl.pallas_call(kernel, out_shape=jax.ShapeDtypeStruct((2, C, D), bf), in_...  38 us

profile of v5, /device:TPU:1, one launch (start us, length us, event | category | flops | bytes accessed | tf_op | source)
XLA Modules:
  0.0 39.5 jit_solution(15511761848418535062)
XLA Ops:
  0.0 0.7 %pad_add_fusion.meta_hbm = s32[17,32]{1,0:T(8,128)S(1)} fusion(s32[1,32]{1,0:T(1,128)} %bitcast.5, s32[16,32]{1,0:T(8,128)} %bitcast.4), kind=kLoop, calls=%fused_computation | loop fusion | flops 544 | bytes 4352 | tf_op jit(solution)/shard_map/concatenate | solution.py:344
  0.7 38.0 %shard_map.73 = bf16[2,128,512]{2,1,0:T(8,128)(2,1)S(1)} custom-call(s32[17,32]{1,0:T(8,128)S(1)} %pad_add_fusion.meta_hbm, bf16[8,4,16,8,512]{4,3,2,1,0:T(8,128)(2,1)} %bitcast.3, bf16[2,128,512]{2,1,0:T(8,128)(2,1)} %cand_hbm.1, bf16[512,1024]{1,0:T(8,128)(2,1)} %kvw_hbm.1, bf16[512,512]{1,0:T(8,128)(2,1)} %qw_hbm.1, bf16[512,512]{1,0:T(8,128)(2,1)} %ow_hbm.1), custom_call_target="tpu_custom_call" | custom-call | tf_op jit(solution)/shard_map/pallas_call | solution.py:312
  38.7 0.7 %copy.9 = bf16[2,128,512]{2,1,0:T(8,128)(2,1)} copy(bf16[2,128,512]{2,1,0:T(8,128)(2,1)S(1)} %shard_map.73) | data formatting | bytes 524288

commit v6 on v5

--- a/solution.py
+++ b/solution.py
@@ -59,19 +59,20 @@
     y, x = c // 4, c % 4
     sibling = (2 * z + 1 - core, c)
 
-    kpos = jnp.where(core == 0, x, y)
-    cpos = jnp.where(core == 0, y, x)
-    kstep = jnp.where(core == 0, 1, 4)
-    cstep = 5 - kstep
-
-    def kdev(d):
-        return (h, cpos * cstep + ((kpos + d) & 3) * kstep)
-
-    def cdev(d):
-        return (h, ((cpos + d) & 3) * cstep + kpos * kstep)
-
-    kpeers = {OPP: kdev(2), LEFT: kdev(1), RIGHT: kdev(3)}
-    cpeers = {OPP: cdev(2), LEFT: cdev(1), RIGHT: cdev(3)}
+    swap = [core, 1 - core]
+    kpos = [jnp.where(w == 0, x, y) for w in swap]
+    cpos = [jnp.where(w == 0, y, x) for w in swap]
+    kstep = [jnp.where(w == 0, 1, 4) for w in swap]
+    cstep = [5 - k for k in kstep]
+
+    def kdev(t, d):
+        return (h, cpos[t] * cstep[t] + ((kpos[t] + d) & 3) * kstep[t])
+
+    def cdev(t, d):
+        return (h, ((cpos[t] + d) & 3) * cstep[t] + kpos[t] * kstep[t])
+
+    kpeers = [{OPP: kdev(t, 2), LEFT: kdev(t, 1), RIGHT: kdev(t, 3)} for t in range(2)]
+    cpeers = [{OPP: cdev(t, 2), LEFT: cdev(t, 1), RIGHT: cdev(t, 3)} for t in range(2)]
 
     hist_copies = [
         pltpu.make_async_copy(hist_hbm.at[:, 2 * (p % 2) + p // 2], hist_v[p], in_sem.at[p]) for p in range(4)
@@ -93,7 +94,7 @@
     for zp in zpeers:
         for k in range(2):
             pl.semaphore_signal(barrier, inc=1, device_id=(2 * zp + k, c), device_id_type=MESH)
-    for dev in [sibling] + [f(d) for f in (kdev, cdev) for d in (2, 1, 3)]:
+    for dev in [sibling] + [f(0, d) for f in (kdev, cdev) for d in (2, 1, 3)]:
         pl.semaphore_signal(barrier, inc=1, device_id=dev, device_id_type=MESH)
 
     for cp in small:
@@ -145,8 +146,8 @@
 
     small[0].wait()
     small[1].wait()
-    rows_to = [spread(gat.at[t], kpeers, xs_sem.at[t], xr_sem.at[t]) for t in range(2)]
-    queries_to = [spread(qall.at[t], cpeers, qs_sem.at[t], qr_sem.at[t]) for t in range(2)]
+    rows_to = [spread(gat.at[t], kpeers[t], xs_sem.at[t], xr_sem.at[t]) for t in range(2)]
+    queries_to = [spread(qall.at[t], cpeers[t], qs_sem.at[t], qr_sem.at[t]) for t in range(2)]
     for t in range(2):
         qall[t, OWN] = jnp.dot(cand_v[t], qw[...], preferred_element_type=jnp.float32).astype(jnp.bfloat16)
         queries_to[t][0]()
@@ -164,7 +165,9 @@
     lane_slot = lax.shift_right_logical(lane, 7)
     lane_n = lax.shift_right_logical(lane, 3) & 15
     lane_k = jnp.where(lane_slot == OPP, 2, jnp.where(lane_slot == LEFT, 3, jnp.where(lane_slot == RIGHT, 1, 0)))
-    lane_row = (cpos * cstep + ((kpos + lane_k) & 3) * kstep) * ROWS + (lane & 7)
+    lane_row = [
+        (cpos[t] * cstep[t] + ((kpos[t] + lane_k) & 3) * kstep[t]) * ROWS + (lane & 7) for t in range(2)
+    ]
     col = lax.broadcasted_iota(jnp.int32, (4 * C, C), 1)
 
     def mask(t):
@@ -172,7 +175,7 @@
         idv = jnp.zeros((1, 4 * C), jnp.int32)
         for n in range(NSEL):
             idv = jnp.where(lane_n == n, sel_ref[n, user], idv)
-        return jnp.where(idv * BLK + lane_row < sel_ref[NSEL, user], 0.0, -1e30).astype(jnp.float32)
+        return jnp.where(idv * BLK + lane_row[t] < sel_ref[NSEL, user], 0.0, -1e30).astype(jnp.float32)
 
     def places(t):
         own = [lax.shift_right_logical(sel_ref[n, 2 * h + t], 4) for n in range(NSEL)]
@@ -207,7 +210,7 @@
             cp = pltpu.make_async_remote_copy(
                 src_ref=osend.at[t, s, heads], dst_ref=orecv.at[t, s, heads],
                 send_sem=os_sem.at[t, s, heads.start], recv_sem=or_sem.at[t, s, heads.start],
-                device_id=cdev(OFFSET[s]), device_id_type=MESH,
+                device_id=cdev(t, OFFSET[s]), device_id_type=MESH,
             )
             cp.start()
             out_copies[t].append(cp)
@@ -217,7 +220,7 @@
             cp = pltpu.make_async_remote_copy(
                 src_ref=ostat.at[t, s, heads], dst_ref=rstat.at[t, s, heads],
                 send_sem=ss_sem.at[t, s, heads.start], recv_sem=sr_sem.at[t, s, heads.start],
-                device_id=cdev(OFFSET[s]), device_id_type=MESH,
+                device_id=cdev(t, OFFSET[s]), device_id_type=MESH,
             )
             cp.start()
             out_copies[t].append(cp)
@@ -277,7 +280,6 @@
     project(0, (OPP,))
     queries_to[0][1](OPP, LEFT, RIGHT)
     attend(0, bias0, lambda hd: None)
-    rows_to[1][2]()
     send_out(0, pl.ds(0, HEADS))
     send_stat(0, pl.ds(0, HEADS))
     project(1, (OWN,))
@@ -297,6 +299,7 @@
     finish(1, True)
 
     rows_to[0][2]()
+    rows_to[1][2]()
     for t in range(2):
         queries_to[t][2]()
         zsent(2 + t)

time: 39.6 us -> 39.6 us (level)
  no operation moved by 1% of the time
where the time goes in v6:
time: 39.6 us; the launch traced here: 39.4 us
  Pallas kernels  38 us (96%)
  other arithmetic  0.72 us (2%)
  local copies, waits for them, and re-layouts  0.71 us (2%)
    pallas_call x1, Pallas kernels, per_device(): pl.pallas_call(kernel, out_shape=jax.ShapeDtypeStruct((2, C, D), bf), in_...  38 us

profile of v6, /device:TPU:1, one launch (start us, length us, event | category | flops | bytes accessed | tf_op | source)
XLA Modules:
  0.0 39.4 jit_solution(10390255981647484996)
XLA Ops:
  0.0 0.7 %pad_add_fusion.meta_hbm = s32[17,32]{1,0:T(8,128)S(1)} fusion(s32[1,32]{1,0:T(1,128)} %bitcast.5, s32[16,32]{1,0:T(8,128)} %bitcast.4), kind=kLoop, calls=%fused_computation | loop fusion | flops 544 | bytes 4352 | tf_op jit(solution)/shard_map/concatenate | solution.py:347
  0.7 38.0 %shard_map.73 = bf16[2,128,512]{2,1,0:T(8,128)(2,1)S(1)} custom-call(s32[17,32]{1,0:T(8,128)S(1)} %pad_add_fusion.meta_hbm, bf16[8,4,16,8,512]{4,3,2,1,0:T(8,128)(2,1)} %bitcast.3, bf16[2,128,512]{2,1,0:T(8,128)(2,1)} %cand_hbm.1, bf16[512,1024]{1,0:T(8,128)(2,1)} %kvw_hbm.1, bf16[512,512]{1,0:T(8,128)(2,1)} %qw_hbm.1, bf16[512,512]{1,0:T(8,128)(2,1)} %ow_hbm.1), custom_call_target="tpu_custom_call" | custom-call | tf_op jit(solution)/shard_map/pallas_call | solution.py:315
  38.7 0.7 %copy.9 = bf16[2,128,512]{2,1,0:T(8,128)(2,1)} copy(bf16[2,128,512]{2,1,0:T(8,128)(2,1)S(1)} %shard_map.73) | data formatting | bytes 524288
